TPU v7x, 32 devices: a whole 2x2x4 slice. The times are simulated.
32 devices in a mesh: sector: 16 (over z, y, core), span: 2 (over x).
Axes of the slice: x: 2, y: 2, z: 4, core: 2. Of those that a mesh axis runs over, the one named last changes fastest.
Arguments:
- rhs: float32 [11, 7, 32, 16, 128], P(None, None, 'sector', 'span'), may hold values from -6 to 6
- diag_coef: float32 [32, 16, 128], P('sector', 'span'), may hold values from 2 to 4
- face_coef: float32 [3, 32, 16, 128], P(None, 'sector', 'span'), may hold values from 0.2 to 0.6
- time_coef: float32 [32, 16, 128], P('sector', 'span'), may hold values from 0.05 to 0.4
- jac_up: float32 [3, 7, 7], replicated, may hold values from -1.5 to 1.5
- jac_down: float32 [3, 7, 7], replicated, may hold values from -1.5 to 1.5
- wall_mask: int32 [32, 16, 128], P('sector', 'span'), may hold values 0 or 1
- stator_adj: float32 [11, 7, 64, 16], P(None, None, 'sector', 'span'), may hold values from -6 to 6
- owner: int32 [11, 32, 16], P(None, 'sector', 'span'), may hold values from 0 to 62, as said below
- first_panel_share: float32 [11, 32, 16], P(None, 'sector', 'span'), may hold values from 0 to 1
Outputs:
- adjoint_out: float32 [11, 7, 32, 16, 128], P(None, None, 'sector', 'span')
- stator_sens: float32 [11, 7, 64, 16], P(None, None, 'sector', 'span')
Inputs may be any that keep to these rules, and one draw needn't show every extreme that they name: For instance t and an inlet cell in azimuthal block b (cells b * 2 to (b + 1) * 2 - 1), owner and owner + 1 both lie in panel block q = (b + (t * 16) // 10 - t // 10) mod 16, that is between q * 4 and (q + 1) * 4 - 1.
All inputs are finite; a program needn't handle non-finite values. No bound on the sum of `wall_mask` on one device may be relied on, other than what follows from the above.
Results may differ from a plain program's by a relative error of at most 0.0001.
Values sent between devices are 32-bit elements; how exact they have to be, the bound alone decides.
No kernel may reach another device: no remote copies, remote signals or barrier semaphores. Data moves between devices by JAX's collectives and lax.ppermute only.
A program may use at most 64 MiB of HBM per device.

v0:
```python
import functools

import jax
import jax.numpy as jnp
import ml_dtypes
import numpy as np
from jax import lax
from jax.experimental import pallas as pl
from jax.experimental.pallas import tpu as pltpu
from jax.sharding import PartitionSpec as P

SWEEPS = 4
LANES = 128
CHUNK = 256
HIGHEST = lax.Precision.HIGHEST
DOWN_AZ, SPECTRAL, UP_SP, DOWN_SP, UP_AX, DOWN_AX, UP_AZ = range(7)
C_TIME, C_AZ, C_SP, C_UP, C_DOWN, C_MASK = range(6)


class Plan:
    def __init__(self, rhs, stator_adj, sectors, spans):
        self.insts, self.fields, self.ct, self.rows, self.nax = rhs.shape
        assert self.ct == 2 and self.nax == LANES
        self.panels = stator_adj.shape[2]
        self.sectors, self.spans = sectors, spans
        self.tf = self.insts * self.fields
        self.pad = -(-self.tf // 16) * 16
        self.cells = self.ct * self.rows
        self.slab = self.rows * LANES
        self.shift = [
            ((t * sectors) // (self.insts - 1) - t // (self.insts - 1)) % sectors for t in range(self.insts)
        ]
        assert len(set(self.shift)) == self.insts
        assert self.slab % CHUNK == 0 and 3 * self.pad <= 256 and self.cells * self.panels <= LANES

    def spectral(self):
        t = np.arange(self.insts)
        off = t[:, None] - t[None, :]
        sines = np.where(off == 0, 1.0, np.sin(np.pi * off / self.insts))
        table = np.where(off == 0, 0.0, 0.5 * (1.0 - 2.0 * (off % 2)) / sines).astype(np.float32)
        full = np.zeros((self.pad, self.pad), np.float32)
        full[: self.tf, : self.tf] = np.kron(table.T, np.eye(self.fields, dtype=np.float32))
        hi = full.astype(ml_dtypes.bfloat16)
        lo = (full - hi.astype(np.float32)).astype(ml_dtypes.bfloat16)
        return np.concatenate([hi, lo, hi], axis=1)

    def field_rows(self):
        out = np.zeros((self.pad, self.fields), np.float32)
        out[np.arange(self.tf), np.arange(self.tf) % self.fields] = 1.0
        return out

    def field_lanes(self):
        return np.tile(self.field_rows().T, (1, 3))

    def block_diagonal(self):
        block = np.full(self.pad, -1)
        block[: self.tf] = np.arange(self.tf) // self.fields
        same = (block[:, None] == block[None, :]) & (block[:, None] >= 0)
        return np.tile(same.astype(np.float32), (1, 3))

    def inst_rows(self):
        out = np.zeros((self.pad, self.insts), np.float32)
        out[np.arange(self.tf), np.arange(self.tf) // self.fields] = 1.0
        return out

    def cell_lanes(self):
        out = np.zeros((self.ct, self.rows, self.ct, self.panels, self.rows), np.float32)
        for a in range(self.ct):
            for r in range(self.rows):
                out[a, r, a, :, r] = 1.0
        return out.reshape(self.cells, -1)

    def panel_lanes(self):
        lane = np.arange(self.cells * self.panels)
        return ((lane // self.rows) % self.panels).astype(np.float32)[None]

    def panel_sum(self):
        return np.tile(np.eye(self.panels * self.rows, dtype=np.float32), (self.ct, 1))


def call(kernel, out, scratch=(), flops=2_000_000, nbytes=1_000_000):
    return pl.pallas_call(
        kernel,
        out_shape=out,
        scratch_shapes=list(scratch),
        compiler_params=pltpu.CompilerParams(vmem_limit_bytes=40 * 1024 * 1024),
        cost_estimate=pl.CostEstimate(flops=flops, bytes_accessed=nbytes, transcendentals=0),
    )


def f32(*shape):
    return jax.ShapeDtypeStruct(shape, jnp.float32)


def split3(x):
    hi = x.astype(jnp.bfloat16)
    lo = (x - hi.astype(jnp.float32)).astype(jnp.bfloat16)
    return jnp.concatenate([hi, hi, lo], axis=0)


def dot3(w, x):
    return jnp.dot(w, split3(x), preferred_element_type=jnp.float32)


def dot_full(a, b):
    return jnp.dot(a, b, precision=HIGHEST, preferred_element_type=jnp.float32)


def lane_index(rows):
    return lax.broadcasted_iota(jnp.int32, (rows, LANES), 1)


def send_panels(plan, stator_ref, out_ref):
    me = lax.axis_index("sector")
    width = plan.panels * plan.rows
    out_ref[...] = jnp.zeros_like(out_ref)
    for t in range(plan.insts):
        to = lax.rem(me + (plan.sectors - plan.shift[t]), plan.sectors)
        out_ref[to, : plan.fields, :width] = stator_ref[t]


def panel_weights(plan, owner_ref, share_ref, inst_rows, cell_lanes, panel_lanes):
    local = lax.rem(owner_ref[...], plan.panels).astype(jnp.float32)
    first = dot_full(dot_full(inst_rows[...], local), cell_lanes[...])
    share = dot_full(dot_full(inst_rows[...], share_ref[...]), cell_lanes[...])
    panel = panel_lanes[...]
    lower = (jnp.abs(first - panel) < 0.5).astype(jnp.float32)
    upper = (jnp.abs(first + 1.0 - panel) < 0.5).astype(jnp.float32)
    return share * lower + (1.0 - share) * upper


def prepare(
    plan, rhs_ref, diag_ref, face_ref, time_ref, mask_ref, got_ref, owner_ref, share_ref,
    inst_rows, cell_lanes, panel_lanes,
    x0_ref, x1_ref, edge_ref, coef_ref, weight_ref, panels_ref,
):
    me = lax.axis_index("sector")
    cells = plan.cells
    scale = mask_ref[...].astype(jnp.float32) / diag_ref[...]
    lane = lane_index(cells)
    coef_ref[C_TIME] = scale * time_ref[...]
    coef_ref[C_AZ] = scale * face_ref[0]
    coef_ref[C_SP] = scale * face_ref[1]
    axial = scale * face_ref[2]
    coef_ref[C_UP] = jnp.where(lane < LANES - 1, axial, 0.0)
    coef_ref[C_DOWN] = jnp.where(lane > 0, axial, 0.0)
    coef_ref[C_MASK] = scale

    weight = panel_weights(plan, owner_ref, share_ref, inst_rows, cell_lanes, panel_lanes)
    weight_ref[...] = weight
    width = plan.panels * plan.rows
    panels_ref[...] = jnp.zeros_like(panels_ref)
    for t in range(plan.insts):
        source = lax.rem(me + plan.shift[t], plan.sectors)
        panels_ref[t * plan.fields : (t + 1) * plan.fields, :width] = got_ref[source, : plan.fields, :width]
    panels = panels_ref[:, :width]
    terms = jnp.concatenate([panels] * plan.ct, axis=1) * weight
    seam = dot_full(terms, jnp.transpose(cell_lanes[...]))
    seam = jnp.concatenate([seam, jnp.zeros((plan.pad, LANES - cells), jnp.float32)], axis=1)

    inlet = lane_index(plan.pad) == 0
    tail = jnp.zeros((plan.pad - plan.tf, LANES), jnp.float32)
    for cell in range(cells):
        a, r = divmod(cell, plan.rows)
        field = jnp.concatenate([rhs_ref[pl.ds(cell, plan.tf, stride=cells), :], tail], axis=0)
        here = pltpu.roll(seam, (LANES - cell) % LANES, axis=1)
        field = (field + jnp.where(inlet, here, 0.0)) * coef_ref[C_MASK, cell : cell + 1, :]
        (x0_ref, x1_ref)[a][:, r * LANES : (r + 1) * LANES] = field
    write_edges(plan, (x0_ref, x1_ref), edge_ref)


def write_edges(plan, x_refs, edge_ref):
    last = plan.slab - LANES
    for a in range(plan.ct):
        low = x_refs[a][:, :LANES]
        high = x_refs[a][:, last:]
        if plan.spans == 2:
            first = lax.axis_index("span") == 0
            edge_ref[0, :, a * LANES : (a + 1) * LANES] = jnp.where(first, high, low)
        else:
            edge_ref[0, :, a * LANES : (a + 1) * LANES] = low
            edge_ref[1, :, a * LANES : (a + 1) * LANES] = high


def stack_matrices(plan, up_ref, down_ref, spectral_ref, rows_ref, lanes_ref, diagonal_ref, out_ref):
    pad = plan.pad
    lane = lax.broadcasted_iota(jnp.int32, (pad, 3 * pad), 1)
    second = (lane >= pad) & (lane < 2 * pad)
    out_ref[SPECTRAL * pad : (SPECTRAL + 1) * pad, :] = spectral_ref[...]
    for block, ref, direction in (
        (DOWN_AZ, down_ref, 0), (UP_SP, up_ref, 1), (DOWN_SP, down_ref, 1),
        (UP_AX, up_ref, 2), (DOWN_AX, down_ref, 2), (UP_AZ, up_ref, 0),
    ):
        full = dot_full(dot_full(rows_ref[...], ref[direction]), lanes_ref[...]) * diagonal_ref[...]
        hi = full.astype(jnp.bfloat16).astype(jnp.float32)
        out_ref[block * pad : (block + 1) * pad, :] = jnp.where(second, full - hi, hi).astype(jnp.bfloat16)


def inner(plan, w_ref, x0_ref, x1_ref, f0_ref, f1_ref, coef_ref, g0_ref, g1_ref, p0_ref, p1_ref):
    pad = plan.pad
    start = (DOWN_AZ, SPECTRAL)
    for a, (x_ref, p_ref) in enumerate(((x0_ref, p0_ref), (x1_ref, p1_ref))):
        for c in range(plan.slab // CHUNK):
            at = slice(c * CHUNK, (c + 1) * CHUNK)
            p_ref[:, at] = dot3(w_ref[start[a] * pad : (start[a] + 6) * pad, :], x_ref[:, at])

    def product(block, a, r):
        row = (block - start[a]) * pad
        return (p0_ref, p1_ref)[a][row : row + pad, r * LANES : (r + 1) * LANES]

    for a in range(plan.ct):
        for r in range(plan.rows):
            cell = a * plan.rows + r

            def coef(which):
                return coef_ref[which, cell : cell + 1, :]

            total = coef(C_TIME) * product(SPECTRAL, a, r)
            other = product(UP_AZ, 1, r) if a == 0 else product(DOWN_AZ, 0, r)
            total = total + coef(C_AZ) * other
            beside = []
            if r + 1 < plan.rows:
                beside.append(product(UP_SP, a, r + 1))
            if r > 0:
                beside.append(product(DOWN_SP, a, r - 1))
            total = total + coef(C_SP) * sum(beside[1:], beside[0])
            total = total + coef(C_UP) * pltpu.roll(product(UP_AX, a, r), LANES - 1, axis=1)
            total = total + coef(C_DOWN) * pltpu.roll(product(DOWN_AX, a, r), 1, axis=1)
            at = slice(r * LANES, (r + 1) * LANES)
            (g0_ref, g1_ref)[a][:, at] = (f0_ref, f1_ref)[a][:, at] - total


def outer_terms(plan, w_ref, low_ref, high_ref, side_ref, coef_ref, g_refs, put):
    pad = plan.pad

    def matrix(block):
        return w_ref[block * pad : (block + 1) * pad, :]

    span = lax.axis_index("span")
    keep_high = jnp.where(span < plan.spans - 1, 1.0, 0.0)
    keep_low = jnp.where(span > 0, 1.0, 0.0)
    above = dot3(matrix(UP_SP), side_ref[0]) * keep_high
    below = dot3(matrix(DOWN_SP), side_ref[side_ref.shape[0] - 1]) * keep_low
    for a, (block, ref) in enumerate(((DOWN_AZ, low_ref), (UP_AZ, high_ref))):
        for c in range(plan.slab // CHUNK):
            terms = dot3(matrix(block), ref[:, c * CHUNK : (c + 1) * CHUNK])
            for part in range(CHUNK // LANES):
                r = c * (CHUNK // LANES) + part
                cell = a * plan.rows + r
                value = g_refs[a][:, r * LANES : (r + 1) * LANES]
                value = value - coef_ref[C_AZ, cell : cell + 1, :] * terms[:, part * LANES : (part + 1) * LANES]
                mine = slice(a * LANES, (a + 1) * LANES)
                if r == 0:
                    value = value - coef_ref[C_SP, cell : cell + 1, :] * below[:, mine]
                if r == plan.rows - 1:
                    value = value - coef_ref[C_SP, cell : cell + 1, :] * above[:, mine]
                put(a, r, value)


def outer(plan, w_ref, low_ref, high_ref, side_ref, coef_ref, g0_ref, g1_ref, x0_ref, x1_ref, edge_ref):
    def put(a, r, value):
        (x0_ref, x1_ref)[a][:, r * LANES : (r + 1) * LANES] = value

    outer_terms(plan, w_ref, low_ref, high_ref, side_ref, coef_ref, (g0_ref, g1_ref), put)
    write_edges(plan, (x0_ref, x1_ref), edge_ref)


def outer_last(
    plan, w_ref, low_ref, high_ref, side_ref, coef_ref, g0_ref, g1_ref, weight_ref, cell_lanes, panel_sum,
    out_ref, send_ref, inlet_ref,
):
    lane = lane_index(plan.pad)
    inlet_ref[...] = jnp.zeros_like(inlet_ref)

    def put(a, r, value):
        cell = a * plan.rows + r
        out_ref[pl.ds(cell, plan.tf, stride=plan.cells), :] = value[: plan.tf]
        inlet_ref[...] = jnp.where(lane == cell, pltpu.roll(value, cell, axis=1) if cell else value, inlet_ref[...])

    outer_terms(plan, w_ref, low_ref, high_ref, side_ref, coef_ref, (g0_ref, g1_ref), put)
    me = lax.axis_index("sector")
    spread = dot_full(inlet_ref[:, : plan.cells], cell_lanes[...]) * weight_ref[...]
    back = dot_full(spread, panel_sum[...])
    width = plan.panels * plan.rows
    send_ref[...] = jnp.zeros_like(send_ref)
    for t in range(plan.insts):
        to = lax.rem(me + plan.shift[t], plan.sectors)
        send_ref[to, : plan.fields, :width] = back[t * plan.fields : (t + 1) * plan.fields]


def collect_panels(plan, got_ref, out_ref):
    me = lax.axis_index("sector")
    width = plan.panels * plan.rows
    for t in range(plan.insts):
        source = lax.rem(me + (plan.sectors - plan.shift[t]), plan.sectors)
        out_ref[t] = got_ref[source, : plan.fields, :width]


def exchange(plan, x0, x1, edge):
    count = plan.sectors
    forward = [(i, (i + 1) % count) for i in range(count)]
    backward = [(target, source) for source, target in forward]
    low = lax.ppermute(x1, "sector", forward)
    high = lax.ppermute(x0, "sector", backward)
    if plan.spans == 2:
        side = lax.ppermute(edge, "span", [(0, 1), (1, 0)])
    else:
        up = [(i, i + 1) for i in range(plan.spans - 1)]
        above = lax.ppermute(edge[0:1], "span", [(target, source) for source, target in up])
        below = lax.ppermute(edge[1:2], "span", up)
        side = jnp.concatenate([above, below], axis=0)
    return low, high, side


def on_device(
    sectors, spans,
    rhs, diag_coef, face_coef, time_coef, jac_up, jac_down, wall_mask, stator_adj, owner, first_panel_share,
):
    plan = Plan(rhs, stator_adj, sectors, spans)
    pad, cells, slab, insts = plan.pad, plan.cells, plan.slab, plan.insts
    width = plan.panels * plan.rows
    edges = 1 if spans == 2 else 2
    bind = functools.partial
    tile = f32(sectors, 8, LANES)
    block = f32(pad, slab)
    edge_shape = f32(edges, pad, plan.ct * LANES)

    sent = call(bind(send_panels, plan), tile)(stator_adj.reshape(insts, plan.fields, width))
    got = lax.all_to_all(sent, "sector", 0, 0, tiled=True)
    cell_lanes = plan.cell_lanes()
    x0, x1, edge, coef, weight = call(
        bind(prepare, plan),
        (block, block, edge_shape, f32(6, cells, LANES), f32(pad, cells * plan.panels)),
        (pltpu.VMEM((pad, LANES), jnp.float32),),
    )(
        rhs.reshape(plan.tf * cells, LANES), diag_coef.reshape(cells, LANES), face_coef.reshape(3, cells, LANES),
        time_coef.reshape(cells, LANES), wall_mask.reshape(cells, LANES), got,
        owner.reshape(insts, cells), first_panel_share.reshape(insts, cells),
        plan.inst_rows(), cell_lanes, plan.panel_lanes(),
    )
    first0, first1 = x0, x1
    matrices = call(
        bind(stack_matrices, plan), jax.ShapeDtypeStruct((7 * pad, 3 * pad), jnp.bfloat16)
    )(jac_up, jac_down, plan.spectral(), plan.field_rows(), plan.field_lanes(), plan.block_diagonal())

    for sweep in range(SWEEPS):
        low, high, side = exchange(plan, x0, x1, edge)
        g0, g1 = call(
            bind(inner, plan), (block, block), (pltpu.VMEM((6 * pad, slab), jnp.float32),) * 2, flops=2_000_000_000
        )(matrices, x0, x1, first0, first1, coef)
        if sweep + 1 < SWEEPS:
            x0, x1, edge = call(bind(outer, plan), (block, block, edge_shape))(
                matrices, low, high, side, coef, g0, g1
            )
    out, sent = call(
        bind(outer_last, plan), (f32(plan.tf * cells, LANES), tile), (pltpu.VMEM((pad, LANES), jnp.float32),)
    )(matrices, low, high, side, coef, g0, g1, weight, cell_lanes, plan.panel_sum())
    got = lax.all_to_all(sent, "sector", 0, 0, tiled=True)
    sens = call(bind(collect_panels, plan), f32(insts, plan.fields, width))(got)
    return out.reshape(rhs.shape), sens.reshape(stator_adj.shape)


def solution(mesh):
    in_specs = (
        P(None, None, "sector", "span", None),
        P("sector", "span", None),
        P(None, "sector", "span", None),
        P("sector", "span", None),
        P(),
        P(),
        P("sector", "span", None),
        P(None, None, "sector", "span"),
        P(None, "sector", "span"),
        P(None, "sector", "span"),
    )
    out_specs = (P(None, None, "sector", "span", None), P(None, None, "sector", "span"))
    return jax.shard_map(
        functools.partial(on_device, mesh.shape["sector"], mesh.shape["span"]),
        mesh=mesh, in_specs=in_specs, out_specs=out_specs, check_vma=False,
    )
```

profile of v0, /device:TPU:0, one launch (start us, length us, event | category | flops | bytes accessed | tf_op | source)
XLA Modules:
  0.0 73.3 jit_solution(14039262330894560658)
XLA Ops:
  0.6 1.0 %copy.28.stator_ref = f32[11,7,32]{2,1,0:T(8,128)S(1)} copy(f32[11,7,32]{0,2,1:T(8,128)} %bitcast.15) | data formatting | bytes 19712 | tf_op jit(solution)/shard_map/reshape | solution.py:328
  2.4 7.5 %all-to-all-start = ((f32[16,8,128]{2,1,0:T(8,128)}), f32[16,8,128]{2,1,0:T(8,128)S(1)}, u32[]{:S(2)}, u32[]{:S(2)}) async-start(f32[16,8,128]{2,1,0:T(8,128)} %shard_map.186), calls=%async_computation | async-start | bytes 131072 | tf_op jit(solution)/shard_map/all_to_all | solution.py:329
  10.1 6.7 %all-to-all-done.got_ref = f32[16,8,128]{2,1,0:T(8,128)S(1)} async-done(((f32[16,8,128]{2,1,0:T(8,128)}), f32[16,8,128]{2,1,0:T(8,128)S(1)}, u32[]{:S(2)}, u32[]{:S(2)}) %all-to-all-start) | async-done | bytes 65568 | tf_op jit(solution)/shard_map/all_to_all | solution.py:329
  17.5 1.1 %copy-done = f32[11,7,2,8,128]{4,3,2,1,0:T(8,128)S(1)} copy-done((f32[11,7,2,8,128]{4,3,2,1,0:T(8,128)S(1)}, f32[11,7,2,8,128]{4,3,2,1,0:T(8,128)}, u32[]{:S(2)}) %copy-start) | copy-done | bytes 630808
  18.6 0.8 %shard_map.187 = (f32[80,1024]{1,0:T(8,128)S(1)}, f32[80,1024]{1,0:T(8,128)S(1)}, f32[1,80,256]{2,1,0:T(8,128)S(1)}, f32[6,16,128]{2,1,0:T(8,128)S(1)}, f32[80,64]{1,0:T(8,128)S(1)}) custom-call(f32[1232,128]{1,0:T(8,128)S(1)} %bitcast.10, f32[16,128]{1,0:T(8,128)S(1)} %bitcast.12, f32[3,16,128]{2,1,0:T(8,128)S(1)} %bitcast.11, f32[16,128]{1,0:T(8,128)S(1)} %bitcast.13, ...), custom_call_target="tpu_custom_call" | custom-call | flops 2000000 | bytes 1000000 | tf_op jit(solution)/shard_map/pallas_call | solution.py:331
  19.5 4.4 %collective-permute-start.1 = (f32[80,1024]{1,0:T(8,128)S(1)}, f32[80,1024]{1,0:T(8,128)S(1)}, u32[]{:S(2)}, u32[]{:S(2)}) collective-permute-start(f32[80,1024]{1,0:T(8,128)S(1)} %get-tuple-element.27.x0_ref.f0_ref), channel_id=1, source_target_pairs={{2,0},{4,2},{6,4},{8,6},{10,8},{12,10},{14,12},{16,14},{18,16},{20... | collective-permute-start | bytes 983048 | tf_op jit(solution)/shard_map/ppermute | solution.py:304
  23.9 1.1 %shard_map.185.w_ref = bf16[560,240]{1,0:T(8,128)(2,1)S(1)} custom-call(f32[3,7,7]{2,1,0:T(8,128)S(1)} %copy-done.8, f32[3,7,7]{2,1,0:T(8,128)S(1)} %copy-done.9, bf16[80,240]{1,0:T(8,128)(2,1)S(1)} %copy-done.4, f32[80,7]{1,0:T(8,128)S(1)} %copy-done.3, f32[7,240]{1,0:T(8,128)S(1)} %copy-done.13, f32[80,240]{1,0:T(8,128)S(1)} %copy-done.1), custom_call_target="tpu_custom_call" | custom-call | flops 2000000 | bytes 1000000 | tf_op jit(solution)/shard_map/pallas_call | solution.py:342
  25.0 1.6 %collective-permute-start.2 = (f32[1,80,256]{2,1,0:T(8,128)S(1)}, f32[1,80,256]{2,1,0:T(8,128)S(1)}, u32[]{:S(2)}, u32[]{:S(2)}) collective-permute-start(f32[1,80,256]{2,1,0:T(8,128)S(1)} %get-tuple-element.28), channel_id=1, source_target_pairs={{0,1},{1,0},{2,3},{3,2},{4,5},{5,4},{6,7},{7,6},{8,9},{9,8},{10,11... | collective-permute-start | bytes 245768 | tf_op jit(solution)/shard_map/ppermute | solution.py:306
  27.4 2.2 %collective-permute-done.2.side_ref = f32[1,80,256]{2,1,0:T(8,128)S(1)} collective-permute-done((f32[1,80,256]{2,1,0:T(8,128)S(1)}, f32[1,80,256]{2,1,0:T(8,128)S(1)}, u32[]{:S(2)}, u32[]{:S(2)}) %collective-permute-start.2) | collective-permute-done | bytes 81952 | tf_op jit(solution)/shard_map/ppermute | solution.py:306
  30.1 4.3 %collective-permute-start.4 = (f32[80,1024]{1,0:T(8,128)S(1)}, f32[80,1024]{1,0:T(8,128)S(1)}, u32[]{:S(2)}, u32[]{:S(2)}) collective-permute-start(f32[80,1024]{1,0:T(8,128)S(1)} %get-tuple-element.33.x0_ref), channel_id=1, source_target_pairs={{2,0},{4,2},{6,4},{8,6},{10,8},{12,10},{14,12},{16,14},{18,16},{20... | collective-permute-start | bytes 983048 | tf_op jit(solution)/shard_map/ppermute | solution.py:304
  34.4 1.5 %collective-permute-start.5 = (f32[1,80,256]{2,1,0:T(8,128)S(1)}, f32[1,80,256]{2,1,0:T(8,128)S(1)}, u32[]{:S(2)}, u32[]{:S(2)}) collective-permute-start(f32[1,80,256]{2,1,0:T(8,128)S(1)} %get-tuple-element.34), channel_id=1, source_target_pairs={{0,1},{1,0},{2,3},{3,2},{4,5},{5,4},{6,7},{7,6},{8,9},{9,8},{10,11... | collective-permute-start | bytes 245768 | tf_op jit(solution)/shard_map/ppermute | solution.py:306
  35.9 0.8 %shard_map.190 = (f32[80,1024]{1,0:T(8,128)S(1)}, f32[80,1024]{1,0:T(8,128)S(1)}) custom-call(bf16[560,240]{1,0:T(8,128)(2,1)S(1)} %shard_map.185.w_ref, f32[80,1024]{1,0:T(8,128)S(1)} %get-tuple-element.33.x0_ref, f32[80,1024]{1,0:T(8,128)S(1)} %get-tuple-element.32.x1_ref, f32[80,1024]{1,0:T(8,128)S(1)} %get-tuple-element.27.x0_ref.f0_ref, ...), custom_call_target="tpu_custom_call" | custom-call | flops 2000000000 | bytes 1000000 | tf_op jit(solution)/shard_map/pallas_call | solution.py:348
  36.7 2.2 %collective-permute-done.5.side_ref = f32[1,80,256]{2,1,0:T(8,128)S(1)} collective-permute-done((f32[1,80,256]{2,1,0:T(8,128)S(1)}, f32[1,80,256]{2,1,0:T(8,128)S(1)}, u32[]{:S(2)}, u32[]{:S(2)}) %collective-permute-start.5) | collective-permute-done | bytes 81952 | tf_op jit(solution)/shard_map/ppermute | solution.py:306
  39.6 1.0 %collective-permute-start.6 = (f32[80,1024]{1,0:T(8,128)S(1)}, f32[80,1024]{1,0:T(8,128)S(1)}, u32[]{:S(2)}, u32[]{:S(2)}) collective-permute-start(f32[80,1024]{1,0:T(8,128)S(1)} %get-tuple-element.37.x1_ref), channel_id=1, source_target_pairs={{0,2},{2,4},{4,6},{6,8},{8,10},{10,12},{12,14},{14,16},{16,18},{18... | collective-permute-start | bytes 983048 | tf_op jit(solution)/shard_map/ppermute | solution.py:303
  40.6 3.6 %collective-permute-start.7 = (f32[80,1024]{1,0:T(8,128)S(1)}, f32[80,1024]{1,0:T(8,128)S(1)}, u32[]{:S(2)}, u32[]{:S(2)}) collective-permute-start(f32[80,1024]{1,0:T(8,128)S(1)} %get-tuple-element.38.x0_ref), channel_id=1, source_target_pairs={{2,0},{4,2},{6,4},{8,6},{10,8},{12,10},{14,12},{16,14},{18,16},{20... | collective-permute-start | bytes 983048 | tf_op jit(solution)/shard_map/ppermute | solution.py:304
  44.2 1.5 %collective-permute-start.8 = (f32[1,80,256]{2,1,0:T(8,128)S(1)}, f32[1,80,256]{2,1,0:T(8,128)S(1)}, u32[]{:S(2)}, u32[]{:S(2)}) collective-permute-start(f32[1,80,256]{2,1,0:T(8,128)S(1)} %get-tuple-element.39), channel_id=1, source_target_pairs={{0,1},{1,0},{2,3},{3,2},{4,5},{5,4},{6,7},{7,6},{8,9},{9,8},{10,11... | collective-permute-start | bytes 245768 | tf_op jit(solution)/shard_map/ppermute | solution.py:306
  46.5 2.2 %collective-permute-done.8.side_ref = f32[1,80,256]{2,1,0:T(8,128)S(1)} collective-permute-done((f32[1,80,256]{2,1,0:T(8,128)S(1)}, f32[1,80,256]{2,1,0:T(8,128)S(1)}, u32[]{:S(2)}, u32[]{:S(2)}) %collective-permute-start.8) | collective-permute-done | bytes 81952 | tf_op jit(solution)/shard_map/ppermute | solution.py:306
  49.3 1.8 %collective-permute-start.9 = (f32[80,1024]{1,0:T(8,128)S(1)}, f32[80,1024]{1,0:T(8,128)S(1)}, u32[]{:S(2)}, u32[]{:S(2)}) collective-permute-start(f32[80,1024]{1,0:T(8,128)S(1)} %get-tuple-element.42.x1_ref), channel_id=1, source_target_pairs={{0,2},{2,4},{4,6},{6,8},{8,10},{10,12},{12,14},{14,16},{16,18},{18... | collective-permute-start | bytes 983048 | tf_op jit(solution)/shard_map/ppermute | solution.py:303
  51.1 2.8 %collective-permute-start.10 = (f32[80,1024]{1,0:T(8,128)S(1)}, f32[80,1024]{1,0:T(8,128)S(1)}, u32[]{:S(2)}, u32[]{:S(2)}) collective-permute-start(f32[80,1024]{1,0:T(8,128)S(1)} %get-tuple-element.43.x0_ref), channel_id=1, source_target_pairs={{2,0},{4,2},{6,4},{8,6},{10,8},{12,10},{14,12},{16,14},{18,16},{20... | collective-permute-start | bytes 983048 | tf_op jit(solution)/shard_map/ppermute | solution.py:304
  53.8 1.5 %collective-permute-start.11 = (f32[1,80,256]{2,1,0:T(8,128)S(1)}, f32[1,80,256]{2,1,0:T(8,128)S(1)}, u32[]{:S(2)}, u32[]{:S(2)}) collective-permute-start(f32[1,80,256]{2,1,0:T(8,128)S(1)} %get-tuple-element.44), channel_id=1, source_target_pairs={{0,1},{1,0},{2,3},{3,2},{4,5},{5,4},{6,7},{7,6},{8,9},{9,8},{10,11... | collective-permute-start | bytes 245768 | tf_op jit(solution)/shard_map/ppermute | solution.py:306
  55.3 0.8 %shard_map.194 = (f32[80,1024]{1,0:T(8,128)S(1)}, f32[80,1024]{1,0:T(8,128)S(1)}) custom-call(bf16[560,240]{1,0:T(8,128)(2,1)S(1)} %shard_map.185.w_ref, f32[80,1024]{1,0:T(8,128)S(1)} %get-tuple-element.43.x0_ref, f32[80,1024]{1,0:T(8,128)S(1)} %get-tuple-element.42.x1_ref, f32[80,1024]{1,0:T(8,128)S(1)} %get-tuple-element.27.x0_ref.f0_ref, ...), custom_call_target="tpu_custom_call" | custom-call | flops 2000000000 | bytes 1000000 | tf_op jit(solution)/shard_map/pallas_call | solution.py:348
  56.1 2.2 %collective-permute-done.11.side_ref = f32[1,80,256]{2,1,0:T(8,128)S(1)} collective-permute-done((f32[1,80,256]{2,1,0:T(8,128)S(1)}, f32[1,80,256]{2,1,0:T(8,128)S(1)}, u32[]{:S(2)}, u32[]{:S(2)}) %collective-permute-start.11) | collective-permute-done | bytes 81952 | tf_op jit(solution)/shard_map/ppermute | solution.py:306
  58.7 1.4 %shard_map.195 = (f32[1232,128]{1,0:T(8,128)}, f32[16,8,128]{2,1,0:T(8,128)S(1)}) custom-call(bf16[560,240]{1,0:T(8,128)(2,1)S(1)} %shard_map.185.w_ref, f32[80,1024]{1,0:T(8,128)S(1)} %collective-permute-done.9.low_ref, f32[80,1024]{1,0:T(8,128)S(1)} %collective-permute-done.10.high_ref, f32[1,80,256]{2,1,0:T(8,128)S(1)} %collective-permute-done.11.side_ref, ...), custom_call_target="tpu_custom_call" | custom-call | flops 2000000 | bytes 1000000 | tf_op jit(solution)/shard_map/pallas_call | solution.py:355
  60.1 12.4 %all_to_all.10.got_ref = f32[16,8,128]{2,1,0:T(8,128)S(1)} all-to-all(f32[16,8,128]{2,1,0:T(8,128)S(1)} %get-tuple-element.49), channel_id=1, replica_groups=mesh['sector'=16,'span'=2] {'sector'}, dimensions={0} | all-to-all | bytes 131072 | tf_op jit(solution)/shard_map/all_to_all | solution.py:358
  (53 shorter events, 6.4 us)
Async XLA Ops:
  2.3 7.6 %copy-start.15 = (s32[11,2,8]{0,2,1:T(8,128)S(1)}, s32[11,2,8]{0,2,1:T(8,128)}, u32[]{:S(2)}) copy-start(s32[11,2,8]{0,2,1:T(8,128)} %param.26) | copy-start | bytes 2116
  2.3 7.7 %copy-start.16 = (f32[11,2,8]{0,2,1:T(8,128)S(1)}, f32[11,2,8]{0,2,1:T(8,128)}, u32[]{:S(2)}) copy-start(f32[11,2,8]{0,2,1:T(8,128)} %param.27) | copy-start | bytes 2116
  2.3 14.5 %copy-start.6 = (f32[16,64]{1,0:T(8,128)S(1)}, f32[16,64]{1,0:T(8,128)}, u32[]{:S(2)}) copy-start(f32[16,64]{1,0:T(8,128)} %constant.17.clone.cell_lanes) | copy-start | bytes 12292
  2.3 14.5 %copy-start.7 = (f32[3,2,8,128]{3,2,1,0:T(8,128)S(1)}, f32[3,2,8,128]{3,2,1,0:T(8,128)}, u32[]{:S(2)}) copy-start(f32[3,2,8,128]{3,2,1,0:T(8,128)} %param.20) | copy-start | bytes 73732
  2.3 14.5 %copy-start.10 = (f32[2,8,128]{2,1,0:T(8,128)S(1)}, f32[2,8,128]{2,1,0:T(8,128)}, u32[]{:S(2)}) copy-start(f32[2,8,128]{2,1,0:T(8,128)} %param.19) | copy-start | bytes 24580
  2.3 14.5 %copy-start.11 = (f32[2,8,128]{2,1,0:T(8,128)S(1)}, f32[2,8,128]{2,1,0:T(8,128)}, u32[]{:S(2)}) copy-start(f32[2,8,128]{2,1,0:T(8,128)} %param.21) | copy-start | bytes 24580
  2.4 14.5 %copy-start.12 = (s32[2,8,128]{2,1,0:T(8,128)S(1)}, s32[2,8,128]{2,1,0:T(8,128)}, u32[]{:S(2)}) copy-start(s32[2,8,128]{2,1,0:T(8,128)} %param.24) | copy-start | bytes 24580
  2.4 14.4 %all-to-all-start = ((f32[16,8,128]{2,1,0:T(8,128)}), f32[16,8,128]{2,1,0:T(8,128)S(1)}, u32[]{:S(2)}, u32[]{:S(2)}) async-start(f32[16,8,128]{2,1,0:T(8,128)} %shard_map.186), calls=%async_computation | async-start | bytes 131072 | tf_op jit(solution)/shard_map/all_to_all | solution.py:329
  9.9 6.9 %copy-start.2 = (f32[80,11]{1,0:T(8,128)S(1)}, f32[80,11]{1,0:T(8,128)}, u32[]{:S(2)}) copy-start(f32[80,11]{1,0:T(8,128)} %constant.16.clone.inst_rows) | copy-start | bytes 10564
  18.5 5.4 %copy-start.4 = (bf16[80,240]{1,0:T(8,128)(2,1)S(1)}, bf16[80,240]{1,0:T(8,128)(2,1)}, u32[]{:S(2)}) copy-start(bf16[80,240]{1,0:T(8,128)(2,1)} %constant.19.clone.spectral_ref) | copy-start | bytes 115204
  18.5 5.4 %copy-start.8 = (f32[3,7,7]{2,1,0:T(8,128)S(1)}, f32[3,7,7]{2,1,0:T(8,128)}, u32[]{:S(2)}) copy-start(f32[3,7,7]{2,1,0:T(8,128)} %up_ref.1) | copy-start | bytes 1768
  18.5 5.4 %copy-start.9 = (f32[3,7,7]{2,1,0:T(8,128)S(1)}, f32[3,7,7]{2,1,0:T(8,128)}, u32[]{:S(2)}) copy-start(f32[3,7,7]{2,1,0:T(8,128)} %down_ref.1) | copy-start | bytes 1768
  19.4 10.1 %collective-permute-start = (f32[80,1024]{1,0:T(8,128)S(1)}, f32[80,1024]{1,0:T(8,128)S(1)}, u32[]{:S(2)}, u32[]{:S(2)}) collective-permute-start(f32[80,1024]{1,0:T(8,128)S(1)} %get-tuple-element.26.x1_ref.f1_ref), channel_id=1, source_target_pairs={{0,2},{2,4},{4,6},{6,8},{8,10},{10,12},{12,14},{14,16},{16,18},{18... | collective-permute-start | bytes 983048 | tf_op jit(solution)/shard_map/ppermute | solution.py:303
  19.5 10.1 %collective-permute-start.1 = (f32[80,1024]{1,0:T(8,128)S(1)}, f32[80,1024]{1,0:T(8,128)S(1)}, u32[]{:S(2)}, u32[]{:S(2)}) collective-permute-start(f32[80,1024]{1,0:T(8,128)S(1)} %get-tuple-element.27.x0_ref.f0_ref), channel_id=1, source_target_pairs={{2,0},{4,2},{6,4},{8,6},{10,8},{12,10},{14,12},{16,14},{18,16},{20... | collective-permute-start | bytes 983048 | tf_op jit(solution)/shard_map/ppermute | solution.py:304
  25.0 4.5 %collective-permute-start.2 = (f32[1,80,256]{2,1,0:T(8,128)S(1)}, f32[1,80,256]{2,1,0:T(8,128)S(1)}, u32[]{:S(2)}, u32[]{:S(2)}) collective-permute-start(f32[1,80,256]{2,1,0:T(8,128)S(1)} %get-tuple-element.28), channel_id=1, source_target_pairs={{0,1},{1,0},{2,3},{3,2},{4,5},{5,4},{6,7},{7,6},{8,9},{9,8},{10,11... | collective-permute-start | bytes 245768 | tf_op jit(solution)/shard_map/ppermute | solution.py:306
  29.9 9.4 %collective-permute-start.3 = (f32[80,1024]{1,0:T(8,128)S(1)}, f32[80,1024]{1,0:T(8,128)S(1)}, u32[]{:S(2)}, u32[]{:S(2)}) collective-permute-start(f32[80,1024]{1,0:T(8,128)S(1)} %get-tuple-element.32.x1_ref), channel_id=1, source_target_pairs={{0,2},{2,4},{4,6},{6,8},{8,10},{10,12},{12,14},{14,16},{16,18},{18... | collective-permute-start | bytes 983048 | tf_op jit(solution)/shard_map/ppermute | solution.py:303
  30.1 9.1 %collective-permute-start.4 = (f32[80,1024]{1,0:T(8,128)S(1)}, f32[80,1024]{1,0:T(8,128)S(1)}, u32[]{:S(2)}, u32[]{:S(2)}) collective-permute-start(f32[80,1024]{1,0:T(8,128)S(1)} %get-tuple-element.33.x0_ref), channel_id=1, source_target_pairs={{2,0},{4,2},{6,4},{8,6},{10,8},{12,10},{14,12},{16,14},{18,16},{20... | collective-permute-start | bytes 983048 | tf_op jit(solution)/shard_map/ppermute | solution.py:304
  34.4 4.4 %collective-permute-start.5 = (f32[1,80,256]{2,1,0:T(8,128)S(1)}, f32[1,80,256]{2,1,0:T(8,128)S(1)}, u32[]{:S(2)}, u32[]{:S(2)}) collective-permute-start(f32[1,80,256]{2,1,0:T(8,128)S(1)} %get-tuple-element.34), channel_id=1, source_target_pairs={{0,1},{1,0},{2,3},{3,2},{4,5},{5,4},{6,7},{7,6},{8,9},{9,8},{10,11... | collective-permute-start | bytes 245768 | tf_op jit(solution)/shard_map/ppermute | solution.py:306
  39.6 9.4 %collective-permute-start.6 = (f32[80,1024]{1,0:T(8,128)S(1)}, f32[80,1024]{1,0:T(8,128)S(1)}, u32[]{:S(2)}, u32[]{:S(2)}) collective-permute-start(f32[80,1024]{1,0:T(8,128)S(1)} %get-tuple-element.37.x1_ref), channel_id=1, source_target_pairs={{0,2},{2,4},{4,6},{6,8},{8,10},{10,12},{12,14},{14,16},{16,18},{18... | collective-permute-start | bytes 983048 | tf_op jit(solution)/shard_map/ppermute | solution.py:303
  40.6 8.4 %collective-permute-start.7 = (f32[80,1024]{1,0:T(8,128)S(1)}, f32[80,1024]{1,0:T(8,128)S(1)}, u32[]{:S(2)}, u32[]{:S(2)}) collective-permute-start(f32[80,1024]{1,0:T(8,128)S(1)} %get-tuple-element.38.x0_ref), channel_id=1, source_target_pairs={{2,0},{4,2},{6,4},{8,6},{10,8},{12,10},{14,12},{16,14},{18,16},{20... | collective-permute-start | bytes 983048 | tf_op jit(solution)/shard_map/ppermute | solution.py:304
  44.2 4.4 %collective-permute-start.8 = (f32[1,80,256]{2,1,0:T(8,128)S(1)}, f32[1,80,256]{2,1,0:T(8,128)S(1)}, u32[]{:S(2)}, u32[]{:S(2)}) collective-permute-start(f32[1,80,256]{2,1,0:T(8,128)S(1)} %get-tuple-element.39), channel_id=1, source_target_pairs={{0,1},{1,0},{2,3},{3,2},{4,5},{5,4},{6,7},{7,6},{8,9},{9,8},{10,11... | collective-permute-start | bytes 245768 | tf_op jit(solution)/shard_map/ppermute | solution.py:306
  49.3 9.4 %collective-permute-start.9 = (f32[80,1024]{1,0:T(8,128)S(1)}, f32[80,1024]{1,0:T(8,128)S(1)}, u32[]{:S(2)}, u32[]{:S(2)}) collective-permute-start(f32[80,1024]{1,0:T(8,128)S(1)} %get-tuple-element.42.x1_ref), channel_id=1, source_target_pairs={{0,2},{2,4},{4,6},{6,8},{8,10},{10,12},{12,14},{14,16},{16,18},{18... | collective-permute-start | bytes 983048 | tf_op jit(solution)/shard_map/ppermute | solution.py:303
  51.1 7.6 %collective-permute-start.10 = (f32[80,1024]{1,0:T(8,128)S(1)}, f32[80,1024]{1,0:T(8,128)S(1)}, u32[]{:S(2)}, u32[]{:S(2)}) collective-permute-start(f32[80,1024]{1,0:T(8,128)S(1)} %get-tuple-element.43.x0_ref), channel_id=1, source_target_pairs={{2,0},{4,2},{6,4},{8,6},{10,8},{12,10},{14,12},{16,14},{18,16},{20... | collective-permute-start | bytes 983048 | tf_op jit(solution)/shard_map/ppermute | solution.py:304
  53.8 4.4 %collective-permute-start.11 = (f32[1,80,256]{2,1,0:T(8,128)S(1)}, f32[1,80,256]{2,1,0:T(8,128)S(1)}, u32[]{:S(2)}, u32[]{:S(2)}) collective-permute-start(f32[1,80,256]{2,1,0:T(8,128)S(1)} %get-tuple-element.44), channel_id=1, source_target_pairs={{0,1},{1,0},{2,3},{3,2},{4,5},{5,4},{6,7},{7,6},{8,9},{9,8},{10,11... | collective-permute-start | bytes 245768 | tf_op jit(solution)/shard_map/ppermute | solution.py:306
  (6 other events, 22.7 us)
where the time goes:
time: 73.7 us; the launch traced here: 73.3 us
  starting transfers between devices  31.6 us (43%)
  waiting for transfers between devices  16.5 us (22%)
  blocking collectives  12.4 us (17%)
  Pallas kernels  8.23 us (11%)
  local copies, waits for them, and re-layouts  3.71 us (5%)
  between operations  0.83 us (1%)
    ppermute x4, starting transfers between devices, exchange(): high = lax.ppermute(x0, 'sector', backward)  15 us
    all_to_all x1, blocking collectives, on_device(): got = lax.all_to_all(sent, 'sector', 0, 0, tiled=True)  12.4 us
    ppermute x4, waiting for transfers between devices, exchange(): side = lax.ppermute(edge, 'span', [(0, 1), (1, 0)])  8.62 us
    all_to_all x1, starting transfers between devices, on_device(): got = lax.all_to_all(sent, 'sector', 0, 0, tiled=True)  7.53 us
    all_to_all x1, waiting for transfers between devices, on_device(): got = lax.all_to_all(sent, 'sector', 0, 0, tiled=True)  6.71 us
    ppermute x4, starting transfers between devices, exchange(): side = lax.ppermute(edge, 'span', [(0, 1), (1, 0)])  6.03 us
    pallas_call x4, Pallas kernels, on_device(): call(bind(inner, plan), (block, block), (pltpu.VMEM((6 * pad, slab), jnp....  3.16 us
    ppermute x4, starting transfers between devices, exchange(): low = lax.ppermute(x1, 'sector', forward)  3 us
  transfers between devices with their start and end apart: 13, of which 8 were waited for; matrix products, arithmetic and copies ran while one was open for 0% of the time, Pallas kernels for 6%

commit v1 on v0

--- a/solution.py
+++ b/solution.py
@@ -12,6 +12,9 @@
 SWEEPS = 4
 LANES = 128
 CHUNK = 256
+WINDOW = 8
+DEPTH = SWEEPS + 1
+SEAM_LANE = 6
 HIGHEST = lax.Precision.HIGHEST
 DOWN_AZ, SPECTRAL, UP_SP, DOWN_SP, UP_AX, DOWN_AX, UP_AZ = range(7)
 C_TIME, C_AZ, C_SP, C_UP, C_DOWN, C_MASK = range(6)
@@ -70,6 +73,13 @@
                 out[a, r, a, :, r] = 1.0
         return out.reshape(self.cells, -1)
 
+    def window_lanes(self):
+        out = np.zeros((self.ct, self.panels, self.rows, self.cells, WINDOW), np.float32)
+        for a in range(self.ct):
+            for r in range(self.rows):
+                out[a, :, r, a * self.rows + r, 0] = 1.0
+        return out.reshape(self.cells * self.panels, LANES)
+
     def panel_lanes(self):
         lane = np.arange(self.cells * self.panels)
         return ((lane // self.rows) % self.panels).astype(np.float32)[None]
@@ -129,12 +139,7 @@
     return share * lower + (1.0 - share) * upper
 
 
-def prepare(
-    plan, rhs_ref, diag_ref, face_ref, time_ref, mask_ref, got_ref, owner_ref, share_ref,
-    inst_rows, cell_lanes, panel_lanes,
-    x0_ref, x1_ref, edge_ref, coef_ref, weight_ref, panels_ref,
-):
-    me = lax.axis_index("sector")
+def prepare(plan, rhs_ref, diag_ref, face_ref, time_ref, mask_ref, x0_ref, x1_ref, edge_ref, coef_ref):
     cells = plan.cells
     scale = mask_ref[...].astype(jnp.float32) / diag_ref[...]
     lane = lane_index(cells)
@@ -145,7 +150,19 @@
     coef_ref[C_UP] = jnp.where(lane < LANES - 1, axial, 0.0)
     coef_ref[C_DOWN] = jnp.where(lane > 0, axial, 0.0)
     coef_ref[C_MASK] = scale
-
+    tail = jnp.zeros((plan.pad - plan.tf, LANES), jnp.float32)
+    for cell in range(cells):
+        a, r = divmod(cell, plan.rows)
+        field = jnp.concatenate([rhs_ref[pl.ds(cell, plan.tf, stride=cells), :], tail], axis=0)
+        (x0_ref, x1_ref)[a][:, r * LANES : (r + 1) * LANES] = field * coef_ref[C_MASK, cell : cell + 1, :]
+    write_edges(plan, (x0_ref, x1_ref), edge_ref)
+
+
+def window_message(
+    plan, got_ref, owner_ref, share_ref, x0_ref, x1_ref, coef_ref, inst_rows, cell_lanes, panel_lanes, window_lanes,
+    message_ref, weight_ref, panels_ref,
+):
+    me = lax.axis_index("sector")
     weight = panel_weights(plan, owner_ref, share_ref, inst_rows, cell_lanes, panel_lanes)
     weight_ref[...] = weight
     width = plan.panels * plan.rows
@@ -153,20 +170,136 @@
     for t in range(plan.insts):
         source = lax.rem(me + plan.shift[t], plan.sectors)
         panels_ref[t * plan.fields : (t + 1) * plan.fields, :width] = got_ref[source, : plan.fields, :width]
-    panels = panels_ref[:, :width]
-    terms = jnp.concatenate([panels] * plan.ct, axis=1) * weight
-    seam = dot_full(terms, jnp.transpose(cell_lanes[...]))
-    seam = jnp.concatenate([seam, jnp.zeros((plan.pad, LANES - cells), jnp.float32)], axis=1)
-
-    inlet = lane_index(plan.pad) == 0
-    tail = jnp.zeros((plan.pad - plan.tf, LANES), jnp.float32)
-    for cell in range(cells):
+    terms = jnp.concatenate([panels_ref[:, :width]] * plan.ct, axis=1) * weight
+    seam = dot_full(terms, window_lanes[...])
+
+    def packed(rows, tile_of):
+        lane = lane_index(rows)
+        out = jnp.zeros((rows, LANES), jnp.float32)
+        for cell in range(plan.cells):
+            at = cell * WINDOW
+            tile = tile_of(cell)
+            tile = pltpu.roll(tile, at, axis=1) if at else tile
+            out = jnp.where((lane >= at) & (lane < at + DEPTH), tile, out)
+        return out
+
+    def field(cell):
         a, r = divmod(cell, plan.rows)
-        field = jnp.concatenate([rhs_ref[pl.ds(cell, plan.tf, stride=cells), :], tail], axis=0)
-        here = pltpu.roll(seam, (LANES - cell) % LANES, axis=1)
-        field = (field + jnp.where(inlet, here, 0.0)) * coef_ref[C_MASK, cell : cell + 1, :]
-        (x0_ref, x1_ref)[a][:, r * LANES : (r + 1) * LANES] = field
-    write_edges(plan, (x0_ref, x1_ref), edge_ref)
+        return (x0_ref, x1_ref)[a][:, r * LANES : (r + 1) * LANES]
+
+    def coefs(cell):
+        return jnp.concatenate([coef_ref[which, cell : cell + 1, :] for which in range(6)] + [zeros], axis=0)
+
+    zeros = jnp.zeros((2, LANES), jnp.float32)
+    rates = packed(8, coefs)
+    seam = seam * rates[C_MASK : C_MASK + 1, :]
+    message_ref[: plan.pad, :] = packed(plan.pad, field) + seam + pltpu.roll(seam, SEAM_LANE, axis=1)
+    message_ref[plan.pad :, :] = rates
+
+
+def window_sweeps(
+    plan, w_ref, *refs
+):
+    sides = 1 if plan.spans == 2 else 2
+    block_refs = refs[:5]
+    side_refs = refs[5 : 5 + sides]
+    weight_ref, window_lanes, panel_sum, inlet_ref, send_ref, force_ref, state_ref, product_ref = refs[5 + sides :]
+    pad, rows = plan.pad, plan.rows
+    span = lax.axis_index("span")
+    keep_high = jnp.where(span < plan.spans - 1, 1.0, 0.0)
+    keep_low = jnp.where(span > 0, 1.0, 0.0)
+    lane = lane_index(pad)
+    cell_at = lax.rem(lane, WINDOW)
+    row_at = lax.rem(lax.div(lane, WINDOW), rows)
+    half = plan.rows * WINDOW
+    blocks, beside = range(-2, 3), range(-1, 2)
+
+    def at(k, x, which):
+        start = (((k + 2) * 3 + x + 1) * 2 + which) * LANES
+        return slice(start, start + LANES)
+
+    def both(k, x):
+        return slice(at(k, x, 0).start, at(k, x, 1).stop)
+
+    rates = {}
+    for k in blocks:
+        for x in beside:
+            if x == 0:
+                message = block_refs[k + 2][...]
+            elif x > 0:
+                message = side_refs[0][k + 2] * keep_high
+            else:
+                message = side_refs[-1][k + 2] * keep_low
+            field = message[:pad]
+            force_ref[:, at(k, x, 0)] = jnp.where(cell_at < DEPTH, field, 0.0)
+            force_ref[:, at(k, x, 1)] = jnp.where(cell_at == 0, pltpu.roll(field, LANES - SEAM_LANE, axis=1), 0.0)
+            rates[k, x] = message[pad:]
+    state_ref[...] = force_ref[...]
+
+    def multiply(k, x, low, high):
+        product_ref[low * pad : high * pad, both(k, x)] = dot3(
+            w_ref[low * pad : high * pad, :], state_ref[:, both(k, x)]
+        )
+
+    def product(block, k, x, which):
+        if k not in blocks or x not in beside:
+            return jnp.zeros((pad, LANES), jnp.float32)
+        return product_ref[block * pad : (block + 1) * pad, at(k, x, which)]
+
+    def rate(which, k, x):
+        return rates[k, x][which : which + 1, :]
+
+    def update(k, x, which):
+        up = pltpu.roll(jnp.where(lane >= half, product(UP_AZ, k, x, which), product(UP_AZ, k + 1, x, which)), half, axis=1)
+        down = pltpu.roll(
+            jnp.where(lane < half, product(DOWN_AZ, k, x, which), product(DOWN_AZ, k - 1, x, which)), half, axis=1
+        )
+        total = rate(C_AZ, k, x) * (up + down)
+        step = (rows - 1) * WINDOW
+        up = jnp.where(
+            row_at < rows - 1,
+            pltpu.roll(product(UP_SP, k, x, which), LANES - WINDOW, axis=1),
+            pltpu.roll(product(UP_SP, k, x + 1, which), step, axis=1),
+        )
+        down = jnp.where(
+            row_at > 0,
+            pltpu.roll(product(DOWN_SP, k, x, which), WINDOW, axis=1),
+            pltpu.roll(product(DOWN_SP, k, x - 1, which), LANES - step, axis=1),
+        )
+        total = total + rate(C_SP, k, x) * (up + down)
+        total = total + rate(C_TIME, k, x) * product(SPECTRAL, k, x, which)
+        total = total + rate(C_UP, k, x) * pltpu.roll(product(UP_AX, k, x, which), LANES - 1, axis=1)
+        total = total + rate(C_DOWN, k, x) * pltpu.roll(product(DOWN_AX, k, x, which), 1, axis=1)
+        state_ref[:, at(k, x, which)] = force_ref[:, at(k, x, which)] - total
+
+    everything = (DOWN_AZ, UP_AZ + 1)
+    for sweep in range(SWEEPS):
+        left = SWEEPS - 1 - sweep
+        reach = -(-left // plan.ct)
+        targets = [(k, x) for k in range(-reach, reach + 1) for x in beside if left or x == 0]
+        for k in blocks:
+            for x in beside:
+                if (k, x) in targets:
+                    multiply(k, x, *everything)
+                elif (k + 1, x) in targets and left % plan.ct == 0:
+                    multiply(k, x, DOWN_AZ, DOWN_AZ + 1)
+                elif (k - 1, x) in targets and left % plan.ct == 0:
+                    multiply(k, x, UP_AZ, UP_AZ + 1)
+                elif (k, x - 1) in targets or (k, x + 1) in targets:
+                    multiply(k, x, UP_SP, DOWN_SP + 1)
+        for k, x in targets:
+            for which in range(2):
+                update(k, x, which)
+    inlet_ref[...] = state_ref[:, at(0, 0, 1)]
+
+    me = lax.axis_index("sector")
+    spread = dot_full(state_ref[:, at(0, 0, 0)], jnp.transpose(window_lanes[...])) * weight_ref[...]
+    back = dot_full(spread, panel_sum[...])
+    width = plan.panels * plan.rows
+    send_ref[...] = jnp.zeros_like(send_ref)
+    for t in range(plan.insts):
+        to = lax.rem(me + plan.shift[t], plan.sectors)
+        send_ref[to, : plan.fields, :width] = back[t * plan.fields : (t + 1) * plan.fields]
 
 
 def write_edges(plan, x_refs, edge_ref):
@@ -265,27 +398,17 @@
     write_edges(plan, (x0_ref, x1_ref), edge_ref)
 
 
-def outer_last(
-    plan, w_ref, low_ref, high_ref, side_ref, coef_ref, g0_ref, g1_ref, weight_ref, cell_lanes, panel_sum,
-    out_ref, send_ref, inlet_ref,
-):
+def outer_last(plan, w_ref, low_ref, high_ref, side_ref, coef_ref, g0_ref, g1_ref, inlet_ref, out_ref):
     lane = lane_index(plan.pad)
-    inlet_ref[...] = jnp.zeros_like(inlet_ref)
 
     def put(a, r, value):
         cell = a * plan.rows + r
+        seam = inlet_ref[...]
+        seam = pltpu.roll(seam, LANES - cell * WINDOW, axis=1) if cell else seam
+        value = value + jnp.where(lane < DEPTH, seam, 0.0)
         out_ref[pl.ds(cell, plan.tf, stride=plan.cells), :] = value[: plan.tf]
-        inlet_ref[...] = jnp.where(lane == cell, pltpu.roll(value, cell, axis=1) if cell else value, inlet_ref[...])
 
     outer_terms(plan, w_ref, low_ref, high_ref, side_ref, coef_ref, (g0_ref, g1_ref), put)
-    me = lax.axis_index("sector")
-    spread = dot_full(inlet_ref[:, : plan.cells], cell_lanes[...]) * weight_ref[...]
-    back = dot_full(spread, panel_sum[...])
-    width = plan.panels * plan.rows
-    send_ref[...] = jnp.zeros_like(send_ref)
-    for t in range(plan.insts):
-        to = lax.rem(me + plan.shift[t], plan.sectors)
-        send_ref[to, : plan.fields, :width] = back[t * plan.fields : (t + 1) * plan.fields]
 
 
 def collect_panels(plan, got_ref, out_ref):
@@ -312,6 +435,23 @@
     return low, high, side
 
 
+def exchange_window(plan, message):
+    count = plan.sectors
+
+    def from_block(k):
+        if k == 0:
+            return message
+        return lax.ppermute(message, "sector", [(i, (i - k) % count) for i in range(count)])
+
+    blocks = [from_block(k) for k in range(-2, 3)]
+    stack = jnp.stack(blocks)
+    if plan.spans == 2:
+        return blocks, [lax.ppermute(stack, "span", [(0, 1), (1, 0)])]
+    up = [(i, i + 1) for i in range(plan.spans - 1)]
+    above = lax.ppermute(stack, "span", [(target, source) for source, target in up])
+    return blocks, [above, lax.ppermute(stack, "span", up)]
+
+
 def on_device(
     sectors, spans,
     rhs, diag_coef, face_coef, time_coef, jac_up, jac_down, wall_mask, stator_adj, owner, first_panel_share,
@@ -327,21 +467,34 @@
 
     sent = call(bind(send_panels, plan), tile)(stator_adj.reshape(insts, plan.fields, width))
     got = lax.all_to_all(sent, "sector", 0, 0, tiled=True)
-    cell_lanes = plan.cell_lanes()
-    x0, x1, edge, coef, weight = call(
-        bind(prepare, plan),
-        (block, block, edge_shape, f32(6, cells, LANES), f32(pad, cells * plan.panels)),
-        (pltpu.VMEM((pad, LANES), jnp.float32),),
-    )(
+    x0, x1, edge, coef = call(bind(prepare, plan), (block, block, edge_shape, f32(6, cells, LANES)))(
         rhs.reshape(plan.tf * cells, LANES), diag_coef.reshape(cells, LANES), face_coef.reshape(3, cells, LANES),
-        time_coef.reshape(cells, LANES), wall_mask.reshape(cells, LANES), got,
-        owner.reshape(insts, cells), first_panel_share.reshape(insts, cells),
-        plan.inst_rows(), cell_lanes, plan.panel_lanes(),
+        time_coef.reshape(cells, LANES), wall_mask.reshape(cells, LANES),
     )
     first0, first1 = x0, x1
     matrices = call(
         bind(stack_matrices, plan), jax.ShapeDtypeStruct((7 * pad, 3 * pad), jnp.bfloat16)
     )(jac_up, jac_down, plan.spectral(), plan.field_rows(), plan.field_lanes(), plan.block_diagonal())
+
+    message, weight = call(
+        bind(window_message, plan), (f32(pad + 8, LANES), f32(pad, cells * plan.panels)),
+        (pltpu.VMEM((pad, LANES), jnp.float32),),
+    )(
+        got, owner.reshape(insts, cells), first_panel_share.reshape(insts, cells), x0, x1, coef,
+        plan.inst_rows(), plan.cell_lanes(), plan.panel_lanes(), plan.window_lanes(),
+    )
+    blocks, beside = exchange_window(plan, message)
+    lanes = 5 * 3 * 2 * LANES
+    inlet, back = call(
+        bind(window_sweeps, plan), (f32(pad, LANES), tile),
+        (
+            pltpu.VMEM((pad, lanes), jnp.float32), pltpu.VMEM((pad, lanes), jnp.float32),
+            pltpu.VMEM((7 * pad, lanes), jnp.float32),
+        ),
+        flops=10_000_000_000,
+    )(matrices, *blocks, *beside, weight, plan.window_lanes(), plan.panel_sum())
+    returned = lax.all_to_all(back, "sector", 0, 0, tiled=True)
+    sens = call(bind(collect_panels, plan), f32(insts, plan.fields, width))(returned)
 
     for sweep in range(SWEEPS):
         low, high, side = exchange(plan, x0, x1, edge)
@@ -352,11 +505,7 @@
             x0, x1, edge = call(bind(outer, plan), (block, block, edge_shape))(
                 matrices, low, high, side, coef, g0, g1
             )
-    out, sent = call(
-        bind(outer_last, plan), (f32(plan.tf * cells, LANES), tile), (pltpu.VMEM((pad, LANES), jnp.float32),)
-    )(matrices, low, high, side, coef, g0, g1, weight, cell_lanes, plan.panel_sum())
-    got = lax.all_to_all(sent, "sector", 0, 0, tiled=True)
-    sens = call(bind(collect_panels, plan), f32(insts, plan.fields, width))(got)
+    out = call(bind(outer_last, plan), f32(plan.tf * cells, LANES))(matrices, low, high, side, coef, g0, g1, inlet)
     return out.reshape(rhs.shape), sens.reshape(stator_adj.shape)
 
 

time: 73.7 us -> 78.4 us (1.064)
  Pallas kernels: 8.23 us -> 14 us
  blocking collectives: 12.4 us -> 9.48 us
    all_to_all x1, waiting for transfers between devices: 6.71 us -> 0.01 us  [on_device(): got = lax.all_to_all(sent, 'sector', 0, 0, tiled=True)]
    ppermute x0 -> x5, waiting for transfers between devices: none -> 6.46 us  [the longest x4 6.45 us: from_block(): lax.ppermute(message, 'sector', [(i, (i - k) % count) for i in range(coun...]
    pallas_call x3 -> x5, Pallas kernels: 2.26 us -> 8.07 us  [the longest x1 5.85 us: on_device(): call(bind(window_sweeps, plan), (f32(pad, LANES), tile), (pltpu.VMEM((pad...]
    all_to_all x1, blocking collectives: 12.4 us -> 9.48 us  [on_device(): returned = lax.all_to_all(back, 'sector', 0, 0, tiled=True)]
    ppermute x0 -> x5, starting transfers between devices: none -> 2.41 us  [the longest x4 1.82 us: from_block(): lax.ppermute(message, 'sector', [(i, (i - k) % count) for i in range(coun...]
    ppermute x4, starting transfers between devices: 6.03 us -> 4.11 us  [exchange(): side = lax.ppermute(edge, 'span', [(0, 1), (1, 0)])]
    ppermute x4, waiting for transfers between devices: 8.62 us -> 10.3 us  [exchange(): side = lax.ppermute(edge, 'span', [(0, 1), (1, 0)])]
    ppermute x4, starting transfers between devices: 3 us -> 1.86 us  [exchange(): low = lax.ppermute(x1, 'sector', forward)]
  transfers between devices with their start and end apart: 13 -> 18, of which waited for: 8 -> 6; matrix products, arithmetic and copies ran while one was open for 0% -> 1% of each run, Pallas kernels for 6% -> 15%
where the time goes in v1:
time: 78.4 us; the launch traced here: 78 us
  starting transfers between devices  32 us (41%)
  waiting for transfers between devices  17.1 us (22%)
  Pallas kernels  14 us (18%)
  blocking collectives  9.48 us (12%)
  local copies, waits for them, and re-layouts  4.39 us (6%)
  between operations  0.95 us (1%)
    ppermute x4, starting transfers between devices, exchange(): high = lax.ppermute(x0, 'sector', backward)  16.1 us
    ppermute x4, waiting for transfers between devices, exchange(): side = lax.ppermute(edge, 'span', [(0, 1), (1, 0)])  10.3 us
    all_to_all x1, blocking collectives, on_device(): returned = lax.all_to_all(back, 'sector', 0, 0, tiled=True)  9.48 us
    all_to_all x1, starting transfers between devices, on_device(): got = lax.all_to_all(sent, 'sector', 0, 0, tiled=True)  7.52 us
    ppermute x4, waiting for transfers between devices, from_block(): lax.ppermute(message, 'sector', [(i, (i - k) % count) for i in range(coun...  6.45 us
    pallas_call x1, Pallas kernels, on_device(): call(bind(window_sweeps, plan), (f32(pad, LANES), tile), (pltpu.VMEM((pad...  5.85 us
    ppermute x4, starting transfers between devices, exchange(): side = lax.ppermute(edge, 'span', [(0, 1), (1, 0)])  4.11 us
    unnamed x41, local copies, waits for them, and re-layouts  3.21 us
  transfers between devices with their start and end apart: 18, of which 6 were waited for; matrix products, arithmetic and copies ran while one was open for 1% of the time, Pallas kernels for 15%

profile of v1, /device:TPU:0, one launch (start us, length us, event | category | flops | bytes accessed | tf_op | source)
XLA Modules:
  0.0 78.0 jit_solution(18438153951890878212)
XLA Ops:
  0.6 1.0 %copy.30.stator_ref = f32[11,7,32]{2,1,0:T(8,128)S(1)} copy(f32[11,7,32]{0,2,1:T(8,128)} %bitcast.26) | data formatting | bytes 19712 | tf_op jit(solution)/shard_map/reshape | solution.py:468
  2.3 7.5 %all-to-all-start = ((f32[16,8,128]{2,1,0:T(8,128)}), f32[16,8,128]{2,1,0:T(8,128)S(1)}, u32[]{:S(2)}, u32[]{:S(2)}) async-start(f32[16,8,128]{2,1,0:T(8,128)} %shard_map.212), calls=%async_computation | async-start | bytes 131072 | tf_op jit(solution)/shard_map/all_to_all | solution.py:469
  10.6 1.1 %copy-done = f32[11,7,2,8,128]{4,3,2,1,0:T(8,128)S(1)} copy-done((f32[11,7,2,8,128]{4,3,2,1,0:T(8,128)S(1)}, f32[11,7,2,8,128]{4,3,2,1,0:T(8,128)}, u32[]{:S(2)}) %copy-start) | copy-done | bytes 630808
  12.4 4.0 %collective-permute-start.1 = (f32[80,1024]{1,0:T(8,128)S(1)}, f32[80,1024]{1,0:T(8,128)S(1)}, u32[]{:S(2)}, u32[]{:S(2)}) collective-permute-start(f32[80,1024]{1,0:T(8,128)S(1)} %get-tuple-element.28.x0_ref.f0_ref), channel_id=1, source_target_pairs={{2,0},{4,2},{6,4},{8,6},{10,8},{12,10},{14,12},{16,14},{18,16},{20... | collective-permute-start | bytes 983048 | tf_op jit(solution)/shard_map/ppermute | solution.py:427
  16.4 1.5 %collective-permute-start.2 = (f32[1,80,256]{2,1,0:T(8,128)S(1)}, f32[1,80,256]{2,1,0:T(8,128)S(1)}, u32[]{:S(2)}, u32[]{:S(2)}) collective-permute-start(f32[1,80,256]{2,1,0:T(8,128)S(1)} %get-tuple-element.29), channel_id=1, source_target_pairs={{0,1},{1,0},{2,3},{3,2},{4,5},{5,4},{6,7},{7,6},{8,9},{9,8},{10,11... | collective-permute-start | bytes 245768 | tf_op jit(solution)/shard_map/ppermute | solution.py:429
  18.2 1.1 %shard_map.203.w_ref = bf16[560,240]{1,0:T(8,128)(2,1)S(1)} custom-call(f32[3,7,7]{2,1,0:T(8,128)S(1)} %copy-done.7, f32[3,7,7]{2,1,0:T(8,128)S(1)} %copy-done.8, bf16[80,240]{1,0:T(8,128)(2,1)S(1)} %copy-done.3, f32[80,7]{1,0:T(8,128)S(1)} %copy-done.4, f32[7,240]{1,0:T(8,128)S(1)} %copy-done.13, f32[80,240]{1,0:T(8,128)S(1)} %copy-done.1), custom_call_target="tpu_custom_call" | custom-call | flops 2000000 | bytes 1000000 | tf_op jit(solution)/shard_map/pallas_call | solution.py:475
  20.7 0.8 %shard_map.205 = (f32[80,1024]{1,0:T(8,128)S(1)}, f32[80,1024]{1,0:T(8,128)S(1)}) custom-call(bf16[560,240]{1,0:T(8,128)(2,1)S(1)} %shard_map.203.w_ref, f32[80,1024]{1,0:T(8,128)S(1)} %get-tuple-element.28.x0_ref.f0_ref, f32[80,1024]{1,0:T(8,128)S(1)} %get-tuple-element.27.x1_ref.f1_ref, f32[80,1024]{1,0:T(8,128)S(1)} %get-tuple-element.28.x0_ref.f0_ref, ...), custom_call_target="tpu_custom_call" | custom-call | flops 2000000000 | bytes 1000000 | tf_op jit(solution)/shard_map/pallas_call | solution.py:501
  21.5 6.2 %collective-permute-done.12.refs_0_ = f32[88,128]{1,0:T(8,128)S(1)} collective-permute-done((f32[88,128]{1,0:T(8,128)S(1)}, f32[88,128]{1,0:T(8,128)S(1)}, u32[]{:S(2)}, u32[]{:S(2)}) %collective-permute-start.12) | collective-permute-done | bytes 45088 | tf_op jit(solution)/shard_map/ppermute | solution.py:444
  28.0 1.7 %collective-permute-start.15 = (f32[88,128]{1,0:T(8,128)S(1)}, f32[88,128]{1,0:T(8,128)S(1)}, u32[]{:S(2)}, u32[]{:S(2)}) collective-permute-start(f32[88,128]{1,0:T(8,128)S(1)} %get-tuple-element.48.refs_2_), channel_id=1, source_target_pairs={{0,28},{2,30},{4,0},{6,2},{8,4},{10,6},{12,8},{14,10},{16,12},{18,... | collective-permute-start | bytes 135176 | tf_op jit(solution)/shard_map/ppermute | solution.py:444
  30.2 4.4 %collective-permute-start.4 = (f32[80,1024]{1,0:T(8,128)S(1)}, f32[80,1024]{1,0:T(8,128)S(1)}, u32[]{:S(2)}, u32[]{:S(2)}) collective-permute-start(f32[80,1024]{1,0:T(8,128)S(1)} %get-tuple-element.34.x0_ref), channel_id=1, source_target_pairs={{2,0},{4,2},{6,4},{8,6},{10,8},{12,10},{14,12},{16,14},{18,16},{20... | collective-permute-start | bytes 983048 | tf_op jit(solution)/shard_map/ppermute | solution.py:427
  35.2 0.8 %shard_map.207 = (f32[80,1024]{1,0:T(8,128)S(1)}, f32[80,1024]{1,0:T(8,128)S(1)}) custom-call(bf16[560,240]{1,0:T(8,128)(2,1)S(1)} %shard_map.203.w_ref, f32[80,1024]{1,0:T(8,128)S(1)} %get-tuple-element.34.x0_ref, f32[80,1024]{1,0:T(8,128)S(1)} %get-tuple-element.33.x1_ref, f32[80,1024]{1,0:T(8,128)S(1)} %get-tuple-element.28.x0_ref.f0_ref, ...), custom_call_target="tpu_custom_call" | custom-call | flops 2000000000 | bytes 1000000 | tf_op jit(solution)/shard_map/pallas_call | solution.py:501
  36.0 3.1 %collective-permute-done.5.side_ref = f32[1,80,256]{2,1,0:T(8,128)S(1)} collective-permute-done((f32[1,80,256]{2,1,0:T(8,128)S(1)}, f32[1,80,256]{2,1,0:T(8,128)S(1)}, u32[]{:S(2)}, u32[]{:S(2)}) %collective-permute-start.5) | collective-permute-done | bytes 81952 | tf_op jit(solution)/shard_map/ppermute | solution.py:429
  39.8 1.2 %collective-permute-start.6 = (f32[80,1024]{1,0:T(8,128)S(1)}, f32[80,1024]{1,0:T(8,128)S(1)}, u32[]{:S(2)}, u32[]{:S(2)}) collective-permute-start(f32[80,1024]{1,0:T(8,128)S(1)} %get-tuple-element.38.x1_ref), channel_id=1, source_target_pairs={{0,2},{2,4},{4,6},{6,8},{8,10},{10,12},{12,14},{14,16},{16,18},{18... | collective-permute-start | bytes 983048 | tf_op jit(solution)/shard_map/ppermute | solution.py:426
  41.0 3.3 %collective-permute-start.7 = (f32[80,1024]{1,0:T(8,128)S(1)}, f32[80,1024]{1,0:T(8,128)S(1)}, u32[]{:S(2)}, u32[]{:S(2)}) collective-permute-start(f32[80,1024]{1,0:T(8,128)S(1)} %get-tuple-element.39.x0_ref), channel_id=1, source_target_pairs={{2,0},{4,2},{6,4},{8,6},{10,8},{12,10},{14,12},{16,14},{18,16},{20... | collective-permute-start | bytes 983048 | tf_op jit(solution)/shard_map/ppermute | solution.py:427
  44.9 1.5 %collective-permute-start.8 = (f32[1,80,256]{2,1,0:T(8,128)S(1)}, f32[1,80,256]{2,1,0:T(8,128)S(1)}, u32[]{:S(2)}, u32[]{:S(2)}) collective-permute-start(f32[1,80,256]{2,1,0:T(8,128)S(1)} %get-tuple-element.40), channel_id=1, source_target_pairs={{0,1},{1,0},{2,3},{3,2},{4,5},{5,4},{6,7},{7,6},{8,9},{9,8},{10,11... | collective-permute-start | bytes 245768 | tf_op jit(solution)/shard_map/ppermute | solution.py:429
  46.4 0.8 %shard_map.209 = (f32[80,1024]{1,0:T(8,128)S(1)}, f32[80,1024]{1,0:T(8,128)S(1)}) custom-call(bf16[560,240]{1,0:T(8,128)(2,1)S(1)} %shard_map.203.w_ref, f32[80,1024]{1,0:T(8,128)S(1)} %get-tuple-element.39.x0_ref, f32[80,1024]{1,0:T(8,128)S(1)} %get-tuple-element.38.x1_ref, f32[80,1024]{1,0:T(8,128)S(1)} %get-tuple-element.28.x0_ref.f0_ref, ...), custom_call_target="tpu_custom_call" | custom-call | flops 2000000000 | bytes 1000000 | tf_op jit(solution)/shard_map/pallas_call | solution.py:501
  47.2 4.0 %collective-permute-done.8.side_ref = f32[1,80,256]{2,1,0:T(8,128)S(1)} collective-permute-done((f32[1,80,256]{2,1,0:T(8,128)S(1)}, f32[1,80,256]{2,1,0:T(8,128)S(1)}, u32[]{:S(2)}, u32[]{:S(2)}) %collective-permute-start.8) | collective-permute-done | bytes 81952 | tf_op jit(solution)/shard_map/ppermute | solution.py:429
  51.8 4.3 %collective-permute-start.10 = (f32[80,1024]{1,0:T(8,128)S(1)}, f32[80,1024]{1,0:T(8,128)S(1)}, u32[]{:S(2)}, u32[]{:S(2)}) collective-permute-start(f32[80,1024]{1,0:T(8,128)S(1)} %get-tuple-element.44.x0_ref), channel_id=1, source_target_pairs={{2,0},{4,2},{6,4},{8,6},{10,8},{12,10},{14,12},{16,14},{18,16},{20... | collective-permute-start | bytes 983048 | tf_op jit(solution)/shard_map/ppermute | solution.py:427
  56.1 5.9 %shard_map.214 = (f32[80,128]{1,0:T(8,128)S(1)}, f32[16,8,128]{2,1,0:T(8,128)S(1)}) custom-call(bf16[560,240]{1,0:T(8,128)(2,1)S(1)} %shard_map.203.w_ref, f32[88,128]{1,0:T(8,128)S(1)} %collective-permute-done.12.refs_0_, f32[88,128]{1,0:T(8,128)S(1)} %collective-permute-done.13.refs_1_, f32[88,128]{1,0:T(8,128)S(1)} %get-tuple-element.48.refs_2_, ...), custom_call_target="tpu_custom_call" | custom-call | flops 10000000000 | bytes 1000000 | tf_op jit(solution)/shard_map/pallas_call | solution.py:488
  62.0 9.5 %all_to_all.10.got_ref = f32[16,8,128]{2,1,0:T(8,128)S(1)} all-to-all(f32[16,8,128]{2,1,0:T(8,128)S(1)} %get-tuple-element.51), channel_id=1, replica_groups=mesh['sector'=16,'span'=2] {'sector'}, dimensions={0} | all-to-all | bytes 131072 | tf_op jit(solution)/shard_map/all_to_all | solution.py:496
  71.5 0.8 copy.31
  72.8 0.8 %shard_map.211 = (f32[80,1024]{1,0:T(8,128)S(1)}, f32[80,1024]{1,0:T(8,128)S(1)}) custom-call(bf16[560,240]{1,0:T(8,128)(2,1)S(1)} %shard_map.203.w_ref, f32[80,1024]{1,0:T(8,128)S(1)} %get-tuple-element.44.x0_ref, f32[80,1024]{1,0:T(8,128)S(1)} %get-tuple-element.43.x1_ref, f32[80,1024]{1,0:T(8,128)S(1)} %get-tuple-element.28.x0_ref.f0_ref, ...), custom_call_target="tpu_custom_call" | custom-call | flops 2000000000 | bytes 1000000 | tf_op jit(solution)/shard_map/pallas_call | solution.py:501
  73.6 3.1 %collective-permute-done.11.side_ref = f32[1,80,256]{2,1,0:T(8,128)S(1)} collective-permute-done((f32[1,80,256]{2,1,0:T(8,128)S(1)}, f32[1,80,256]{2,1,0:T(8,128)S(1)}, u32[]{:S(2)}, u32[]{:S(2)}) %collective-permute-start.11) | collective-permute-done | bytes 81952 | tf_op jit(solution)/shard_map/ppermute | solution.py:429
  76.7 1.3 %shard_map.215 = f32[1232,128]{1,0:T(8,128)} custom-call(bf16[560,240]{1,0:T(8,128)(2,1)S(1)} %shard_map.203.w_ref, f32[80,1024]{1,0:T(8,128)S(1)} %collective-permute-done.9.low_ref, f32[80,1024]{1,0:T(8,128)S(1)} %collective-permute-done.10.high_ref, f32[1,80,256]{2,1,0:T(8,128)S(1)} %collective-permute-done.11.side_ref, ...), custom_call_target="tpu_custom_call" | custom-call | flops 2000000 | bytes 1000000 | tf_op jit(solution)/shard_map/pallas_call | solution.py:508
  (72 shorter events, 7.3 us)
Async XLA Ops:
  2.3 7.5 %copy-start.6 = (f32[3,2,8,128]{3,2,1,0:T(8,128)S(1)}, f32[3,2,8,128]{3,2,1,0:T(8,128)}, u32[]{:S(2)}) copy-start(f32[3,2,8,128]{3,2,1,0:T(8,128)} %param.22) | copy-start | bytes 73732
  2.3 7.6 %copy-start.10 = (f32[2,8,128]{2,1,0:T(8,128)S(1)}, f32[2,8,128]{2,1,0:T(8,128)}, u32[]{:S(2)}) copy-start(f32[2,8,128]{2,1,0:T(8,128)} %param.23) | copy-start | bytes 24580
  2.3 7.6 %copy-start.11 = (s32[2,8,128]{2,1,0:T(8,128)S(1)}, s32[2,8,128]{2,1,0:T(8,128)}, u32[]{:S(2)}) copy-start(s32[2,8,128]{2,1,0:T(8,128)} %param.26) | copy-start | bytes 24580
  2.3 17.0 %all-to-all-start = ((f32[16,8,128]{2,1,0:T(8,128)}), f32[16,8,128]{2,1,0:T(8,128)S(1)}, u32[]{:S(2)}, u32[]{:S(2)}) async-start(f32[16,8,128]{2,1,0:T(8,128)} %shard_map.212), calls=%async_computation | async-start | bytes 131072 | tf_op jit(solution)/shard_map/all_to_all | solution.py:469
  11.6 6.5 %copy-start.1 = (f32[80,240]{1,0:T(8,128)S(1)}, f32[80,240]{1,0:T(8,128)}, u32[]{:S(2)}) copy-start(f32[80,240]{1,0:T(8,128)} %constant.21.clone.diagonal_ref) | copy-start | bytes 230404
  11.6 6.5 %copy-start.4 = (f32[80,7]{1,0:T(8,128)S(1)}, f32[80,7]{1,0:T(8,128)}, u32[]{:S(2)}) copy-start(f32[80,7]{1,0:T(8,128)} %constant.19.clone.rows_ref) | copy-start | bytes 6724
  11.6 6.5 %copy-start.7 = (f32[3,7,7]{2,1,0:T(8,128)S(1)}, f32[3,7,7]{2,1,0:T(8,128)}, u32[]{:S(2)}) copy-start(f32[3,7,7]{2,1,0:T(8,128)} %up_ref.1) | copy-start | bytes 1768
  11.9 17.8 %collective-permute-start = (f32[80,1024]{1,0:T(8,128)S(1)}, f32[80,1024]{1,0:T(8,128)S(1)}, u32[]{:S(2)}, u32[]{:S(2)}) collective-permute-start(f32[80,1024]{1,0:T(8,128)S(1)} %get-tuple-element.27.x1_ref.f1_ref), channel_id=1, source_target_pairs={{0,2},{2,4},{4,6},{6,8},{8,10},{10,12},{12,14},{14,16},{16,18},{18... | collective-permute-start | bytes 983048 | tf_op jit(solution)/shard_map/ppermute | solution.py:426
  12.4 17.3 %collective-permute-start.1 = (f32[80,1024]{1,0:T(8,128)S(1)}, f32[80,1024]{1,0:T(8,128)S(1)}, u32[]{:S(2)}, u32[]{:S(2)}) collective-permute-start(f32[80,1024]{1,0:T(8,128)S(1)} %get-tuple-element.28.x0_ref.f0_ref), channel_id=1, source_target_pairs={{2,0},{4,2},{6,4},{8,6},{10,8},{12,10},{14,12},{16,14},{18,16},{20... | collective-permute-start | bytes 983048 | tf_op jit(solution)/shard_map/ppermute | solution.py:427
  16.4 13.3 %collective-permute-start.2 = (f32[1,80,256]{2,1,0:T(8,128)S(1)}, f32[1,80,256]{2,1,0:T(8,128)S(1)}, u32[]{:S(2)}, u32[]{:S(2)}) collective-permute-start(f32[1,80,256]{2,1,0:T(8,128)S(1)} %get-tuple-element.29), channel_id=1, source_target_pairs={{0,1},{1,0},{2,3},{3,2},{4,5},{5,4},{6,7},{7,6},{8,9},{9,8},{10,11... | collective-permute-start | bytes 245768 | tf_op jit(solution)/shard_map/ppermute | solution.py:429
  20.6 7.1 %collective-permute-start.12 = (f32[88,128]{1,0:T(8,128)S(1)}, f32[88,128]{1,0:T(8,128)S(1)}, u32[]{:S(2)}, u32[]{:S(2)}) collective-permute-start(f32[88,128]{1,0:T(8,128)S(1)} %get-tuple-element.48.refs_2_), channel_id=1, source_target_pairs={{0,4},{2,6},{4,8},{6,10},{8,12},{10,14},{12,16},{14,18},{16,20},{1... | collective-permute-start | bytes 135176 | tf_op jit(solution)/shard_map/ppermute | solution.py:444
  21.5 6.5 %collective-permute-start.13 = (f32[88,128]{1,0:T(8,128)S(1)}, f32[88,128]{1,0:T(8,128)S(1)}, u32[]{:S(2)}, u32[]{:S(2)}) collective-permute-start(f32[88,128]{1,0:T(8,128)S(1)} %get-tuple-element.48.refs_2_), channel_id=1, source_target_pairs={{0,2},{2,4},{4,6},{6,8},{8,10},{10,12},{12,14},{14,16},{16,18},{18... | collective-permute-start | bytes 135176 | tf_op jit(solution)/shard_map/ppermute | solution.py:444
  27.7 6.9 %collective-permute-start.14 = (f32[88,128]{1,0:T(8,128)S(1)}, f32[88,128]{1,0:T(8,128)S(1)}, u32[]{:S(2)}, u32[]{:S(2)}) collective-permute-start(f32[88,128]{1,0:T(8,128)S(1)} %get-tuple-element.48.refs_2_), channel_id=1, source_target_pairs={{0,30},{2,0},{4,2},{6,4},{8,6},{10,8},{12,10},{14,12},{16,14},{18,... | collective-permute-start | bytes 135176 | tf_op jit(solution)/shard_map/ppermute | solution.py:444
  28.0 16.3 %collective-permute-start.15 = (f32[88,128]{1,0:T(8,128)S(1)}, f32[88,128]{1,0:T(8,128)S(1)}, u32[]{:S(2)}, u32[]{:S(2)}) collective-permute-start(f32[88,128]{1,0:T(8,128)S(1)} %get-tuple-element.48.refs_2_), channel_id=1, source_target_pairs={{0,28},{2,30},{4,0},{6,2},{8,4},{10,6},{12,8},{14,10},{16,12},{18,... | collective-permute-start | bytes 135176 | tf_op jit(solution)/shard_map/ppermute | solution.py:444
  30.1 9.4 %collective-permute-start.3 = (f32[80,1024]{1,0:T(8,128)S(1)}, f32[80,1024]{1,0:T(8,128)S(1)}, u32[]{:S(2)}, u32[]{:S(2)}) collective-permute-start(f32[80,1024]{1,0:T(8,128)S(1)} %get-tuple-element.33.x1_ref), channel_id=1, source_target_pairs={{0,2},{2,4},{4,6},{6,8},{8,10},{10,12},{12,14},{14,16},{16,18},{18... | collective-permute-start | bytes 983048 | tf_op jit(solution)/shard_map/ppermute | solution.py:426
  30.2 9.3 %collective-permute-start.4 = (f32[80,1024]{1,0:T(8,128)S(1)}, f32[80,1024]{1,0:T(8,128)S(1)}, u32[]{:S(2)}, u32[]{:S(2)}) collective-permute-start(f32[80,1024]{1,0:T(8,128)S(1)} %get-tuple-element.34.x0_ref), channel_id=1, source_target_pairs={{2,0},{4,2},{6,4},{8,6},{10,8},{12,10},{14,12},{16,14},{18,16},{20... | collective-permute-start | bytes 983048 | tf_op jit(solution)/shard_map/ppermute | solution.py:427
  34.6 4.5 %collective-permute-start.5 = (f32[1,80,256]{2,1,0:T(8,128)S(1)}, f32[1,80,256]{2,1,0:T(8,128)S(1)}, u32[]{:S(2)}, u32[]{:S(2)}) collective-permute-start(f32[1,80,256]{2,1,0:T(8,128)S(1)} %get-tuple-element.35), channel_id=1, source_target_pairs={{0,1},{1,0},{2,3},{3,2},{4,5},{5,4},{6,7},{7,6},{8,9},{9,8},{10,11... | collective-permute-start | bytes 245768 | tf_op jit(solution)/shard_map/ppermute | solution.py:429
  39.8 11.4 %collective-permute-start.6 = (f32[80,1024]{1,0:T(8,128)S(1)}, f32[80,1024]{1,0:T(8,128)S(1)}, u32[]{:S(2)}, u32[]{:S(2)}) collective-permute-start(f32[80,1024]{1,0:T(8,128)S(1)} %get-tuple-element.38.x1_ref), channel_id=1, source_target_pairs={{0,2},{2,4},{4,6},{6,8},{8,10},{10,12},{12,14},{14,16},{16,18},{18... | collective-permute-start | bytes 983048 | tf_op jit(solution)/shard_map/ppermute | solution.py:426
  41.0 10.3 %collective-permute-start.7 = (f32[80,1024]{1,0:T(8,128)S(1)}, f32[80,1024]{1,0:T(8,128)S(1)}, u32[]{:S(2)}, u32[]{:S(2)}) collective-permute-start(f32[80,1024]{1,0:T(8,128)S(1)} %get-tuple-element.39.x0_ref), channel_id=1, source_target_pairs={{2,0},{4,2},{6,4},{8,6},{10,8},{12,10},{14,12},{16,14},{18,16},{20... | collective-permute-start | bytes 983048 | tf_op jit(solution)/shard_map/ppermute | solution.py:427
  44.3 11.8 %collective-permute-start.16 = (f32[5,88,128]{2,1,0:T(8,128)S(1)}, f32[5,88,128]{2,1,0:T(8,128)S(1)}, u32[]{:S(2)}, u32[]{:S(2)}) collective-permute-start(f32[5,88,128]{2,1,0:T(8,128)S(1)} %bitcast_dynamic-update-slice_fusion), channel_id=1, source_target_pairs={{0,1},{1,0},{2,3},{3,2},{4,5},{5,4},{6,7},{7,6},{8,9},{9,8},{10,11... | collective-permute-start | bytes 675848 | tf_op jit(solution)/shard_map/ppermute | solution.py:449
  44.9 6.3 %collective-permute-start.8 = (f32[1,80,256]{2,1,0:T(8,128)S(1)}, f32[1,80,256]{2,1,0:T(8,128)S(1)}, u32[]{:S(2)}, u32[]{:S(2)}) collective-permute-start(f32[1,80,256]{2,1,0:T(8,128)S(1)} %get-tuple-element.40), channel_id=1, source_target_pairs={{0,1},{1,0},{2,3},{3,2},{4,5},{5,4},{6,7},{7,6},{8,9},{9,8},{10,11... | collective-permute-start | bytes 245768 | tf_op jit(solution)/shard_map/ppermute | solution.py:429
  51.6 25.1 %collective-permute-start.9 = (f32[80,1024]{1,0:T(8,128)S(1)}, f32[80,1024]{1,0:T(8,128)S(1)}, u32[]{:S(2)}, u32[]{:S(2)}) collective-permute-start(f32[80,1024]{1,0:T(8,128)S(1)} %get-tuple-element.43.x1_ref), channel_id=1, source_target_pairs={{0,2},{2,4},{4,6},{6,8},{8,10},{10,12},{12,14},{14,16},{16,18},{18... | collective-permute-start | bytes 983048 | tf_op jit(solution)/shard_map/ppermute | solution.py:426
  51.8 24.9 %collective-permute-start.10 = (f32[80,1024]{1,0:T(8,128)S(1)}, f32[80,1024]{1,0:T(8,128)S(1)}, u32[]{:S(2)}, u32[]{:S(2)}) collective-permute-start(f32[80,1024]{1,0:T(8,128)S(1)} %get-tuple-element.44.x0_ref), channel_id=1, source_target_pairs={{2,0},{4,2},{6,4},{8,6},{10,8},{12,10},{14,12},{16,14},{18,16},{20... | collective-permute-start | bytes 983048 | tf_op jit(solution)/shard_map/ppermute | solution.py:427
  72.2 4.4 %collective-permute-start.11 = (f32[1,80,256]{2,1,0:T(8,128)S(1)}, f32[1,80,256]{2,1,0:T(8,128)S(1)}, u32[]{:S(2)}, u32[]{:S(2)}) collective-permute-start(f32[1,80,256]{2,1,0:T(8,128)S(1)} %get-tuple-element.45), channel_id=1, source_target_pairs={{0,1},{1,0},{2,3},{3,2},{4,5},{5,4},{6,7},{7,6},{8,9},{9,8},{10,11... | collective-permute-start | bytes 245768 | tf_op jit(solution)/shard_map/ppermute | solution.py:429
  (12 other events, 42.5 us)
